TPU v7x, 256 devices: a whole 4x4x8 slice. The times are simulated.
256 devices in a mesh: shard: 32 (over z, y), rep: 8 (over x, core).
Axes of the slice: x: 4, y: 4, z: 8, core: 2. Of those that a mesh axis runs over, the one named last changes fastest.
Arguments:
- queries: bfloat16 [1024, 32, 128], P(('shard', 'rep')), may hold values from -1.796875 to 1.796875
- passages: bfloat16 [8192, 72, 128], P('shard'), may hold values from -1.796875 to 1.796875
- cand_rows: int32 [1024, 32, 32], P(('shard', 'rep')), may hold values from 0 to 255
- cand_counts: int32 [1024, 32], P(('shard', 'rep')), may hold values from 0 to 32, as said below
Outputs:
- scores: float32 [1024, 32, 32], P(('shard', 'rep'))
Inputs may be any that keep to these rules, and one draw needn't show every extreme that they name: `cand_rows`: slots at or past the count hold rows that are not used. `cand_counts`: some query has 32 live slots in some shard in every draw.
All inputs are finite; a program needn't handle non-finite values.
Results may differ from a plain program's by a relative error of at most 0.0003.
Values may be sent and summed in bfloat16 or wider, within the bound.
A program may use at most 64 MiB of HBM per device.

v0:
```python
import jax
import jax.numpy as jnp
from jax import lax
from jax.sharding import PartitionSpec as P

PLEN = 70


def score_group(pair, passages):
    query_grp, row_grp = pair
    picked = jnp.take(passages, row_grp, axis=0)
    sims = jnp.einsum("ntd,ncpd->nctp", query_grp, picked, preferred_element_type=jnp.float32)
    valid = jnp.arange(passages.shape[1]) < PLEN
    sims = jnp.where(valid[None, None, None, :], sims, -jnp.inf)
    best = jnp.max(sims, axis=-1)
    return jnp.mean(best, axis=-1)


def score_rows(query_tok, rows, passages):
    count = query_tok.shape[0]
    groups = count // 8
    query_grp = query_tok.reshape(groups, 8, query_tok.shape[1], query_tok.shape[2])
    row_grp = rows.reshape(groups, 8, rows.shape[1])
    values = lax.map(lambda pair: score_group(pair, passages), (query_grp, row_grp))
    return values.reshape(count, rows.shape[1])


def score_slots(query_tok, rows, passages):
    return score_rows(query_tok, rows, passages)


def body(queries, passages, cand_rows, cand_counts):
    capacity = cand_rows.shape[2]
    everyone = lax.all_gather(queries, "shard", axis=0, tiled=True)
    arrived, arrived_counts = (
        lax.all_to_all(cand_rows, "shard", split_axis=1, concat_axis=0, tiled=True),
        lax.all_to_all(cand_counts, "shard", split_axis=1, concat_axis=0, tiled=True),
    )
    values = score_slots(everyone, arrived[:, 0, :], passages)
    returned = lax.all_to_all(values[:, None, :], "shard", split_axis=0, concat_axis=1, tiled=True)
    slots = jnp.arange(capacity)
    live = slots[None, None, :] < cand_counts[:, :, None]
    return jnp.where(live, returned, jnp.float32(0.0))


def solution(mesh):
    return jax.shard_map(
        body,
        mesh=mesh,
        in_specs=(
            P(("shard", "rep"), None, None),
            P("shard", None, None),
            P(("shard", "rep"), None, None),
            P(("shard", "rep"), None),
        ),
        out_specs=P(("shard", "rep"), None, None),
        check_vma=False,
    )
```

profile of v0, /device:TPU:4, one launch (start us, length us, event | category | flops | bytes accessed | tf_op | source)
XLA Modules:
  0.0 314.8 jit_solution(4137541053858929308)
XLA Ops:
  6.5 0.7 all-gather.2.cloned.1.call-update
  7.3 0.9 copy.17
  8.1 0.7 reshape.63
  8.9 11.5 %all-to-all-start = ((s32[32,1,128]{2,1,0:T(1,128)}), s32[32,1,128]{2,1,0:T(1,128)S(1)}, u32[]{:S(2)}, u32[]{:S(2)}) async-start(s32[32,1,128]{2,1,0:T(1,128)} %reshape.63), calls=%async_computation | async-start | bytes 32768 | tf_op jit(solution)/shard_map/all_to_all | solution.py:36
  20.4 9.6 %all-to-all-done = s32[32,1,128]{2,1,0:T(1,128)S(1)} async-done(((s32[32,1,128]{2,1,0:T(1,128)}), s32[32,1,128]{2,1,0:T(1,128)S(1)}, u32[]{:S(2)}, u32[]{:S(2)}) %all-to-all-start) | async-done | bytes 16416 | tf_op jit(solution)/shard_map/all_to_all | solution.py:36
  30.0 0.5 broadcast.54
  30.5 0.7 reduce.1
  31.3 57.8 %all-gather.2.cloned.1.call-done = bf16[128,32,128]{2,1,0:T(8,128)(2,1)} async-done(((bf16[4,32,128]{2,1,0:T(8,128)(2,1)}), bf16[128,32,128]{2,1,0:T(8,128)(2,1)}) %all-gather.2.cloned.1.call-update) | async-done | bytes 1048592 | tf_op jit(solution)/shard_map/all_gather | solution.py:34
  89.1 199.2 %while.10 = (s32[]{:T(128)}, f32[16,8,32]{2,1,0:T(8,128)S(1)}, s32[16,8,32]{2,1,0:T(8,128)S(1)}, bf16[256,72,128]{2,1,0:T(8,128)(2,1)}, bf16[16,8,32,128]{3,2,1,0:T(8,128)(2,1)}, /*index=5*/s32[]{:T(128)}, f32[]{:T(128)}) while((s32[]{:T(128)}, f32[16,8,32]{2,1,0:T(8,128)S(1)}, s32[16,8,32]{2,1,0:T(8,128)S(1)}, ...), condition=%wide.region_3.4_spmd, body=%wide.region_0.3_spmd.sunk | while | flops 154537296 | bytes 14308589 | solution.py:24
  89.2 5.7 %gather_fusion = bf16[256,72,128]{2,1,0:T(8,128)(2,1)} fusion(bf16[256,72,128]{2,1,0:T(8,128)(2,1)} %get-tuple-element.91, s32[1024]{0:T(1024)S(1)} %pad_clamp_fusion.2), kind=kCustom, calls=%fused_computation.clone.1 | custom fusion | bytes 9438208 | tf_op jit(solution)/shard_map/while/body/eval_jaxpr/jit(_take)/gather | solution.py:11
  94.9 6.5 %select_reduce_fusion.2 = f32[8,32,32]{2,1,0:T(8,128)S(1)} fusion(pred[72]{0:T(512)(128)(4,1)S(1)} %iota_compare_fusion.3, bf16[8,32,72,128]{3,2,1,0:T(8,128)(2,1)} %bitcast.43, pred[8,32]{1,0:T(8,128)(4,1)S(1)} %compare_and_fusion.2, bf16[16,8,32,128]{3,2,1,0:T(8,128)(2,1)} %get-tuple-element.92, s32[]{:T(128)} %get-tuple-element.81), kind=kOutput, calls=%fused_computation.4.clone.1 | convolution fusion | flops 154525696 | bytes 4817736 | tf_op jit(solution)/shard_map/while/body/eval_jaxpr/ntd,ncpd->nctp/dot_general | solution.py:12
  101.7 5.7 %gather_fusion = bf16[256,72,128]{2,1,0:T(8,128)(2,1)} fusion(bf16[256,72,128]{2,1,0:T(8,128)(2,1)} %get-tuple-element.91, s32[1024]{0:T(1024)S(1)} %pad_clamp_fusion.2), kind=kCustom, calls=%fused_computation.clone.1 | custom fusion | bytes 9438208 | tf_op jit(solution)/shard_map/while/body/eval_jaxpr/jit(_take)/gather | solution.py:11
  107.4 6.5 %select_reduce_fusion.2 = f32[8,32,32]{2,1,0:T(8,128)S(1)} fusion(pred[72]{0:T(512)(128)(4,1)S(1)} %iota_compare_fusion.3, bf16[8,32,72,128]{3,2,1,0:T(8,128)(2,1)} %bitcast.43, pred[8,32]{1,0:T(8,128)(4,1)S(1)} %compare_and_fusion.2, bf16[16,8,32,128]{3,2,1,0:T(8,128)(2,1)} %get-tuple-element.92, s32[]{:T(128)} %get-tuple-element.81), kind=kOutput, calls=%fused_computation.4.clone.1 | convolution fusion | flops 154525696 | bytes 4817736 | tf_op jit(solution)/shard_map/while/body/eval_jaxpr/ntd,ncpd->nctp/dot_general | solution.py:12
  114.1 5.7 %gather_fusion = bf16[256,72,128]{2,1,0:T(8,128)(2,1)} fusion(bf16[256,72,128]{2,1,0:T(8,128)(2,1)} %get-tuple-element.91, s32[1024]{0:T(1024)S(1)} %pad_clamp_fusion.2), kind=kCustom, calls=%fused_computation.clone.1 | custom fusion | bytes 9438208 | tf_op jit(solution)/shard_map/while/body/eval_jaxpr/jit(_take)/gather | solution.py:11
  119.8 6.5 %select_reduce_fusion.2 = f32[8,32,32]{2,1,0:T(8,128)S(1)} fusion(pred[72]{0:T(512)(128)(4,1)S(1)} %iota_compare_fusion.3, bf16[8,32,72,128]{3,2,1,0:T(8,128)(2,1)} %bitcast.43, pred[8,32]{1,0:T(8,128)(4,1)S(1)} %compare_and_fusion.2, bf16[16,8,32,128]{3,2,1,0:T(8,128)(2,1)} %get-tuple-element.92, s32[]{:T(128)} %get-tuple-element.81), kind=kOutput, calls=%fused_computation.4.clone.1 | convolution fusion | flops 154525696 | bytes 4817736 | tf_op jit(solution)/shard_map/while/body/eval_jaxpr/ntd,ncpd->nctp/dot_general | solution.py:12
  126.6 5.7 %gather_fusion = bf16[256,72,128]{2,1,0:T(8,128)(2,1)} fusion(bf16[256,72,128]{2,1,0:T(8,128)(2,1)} %get-tuple-element.91, s32[1024]{0:T(1024)S(1)} %pad_clamp_fusion.2), kind=kCustom, calls=%fused_computation.clone.1 | custom fusion | bytes 9438208 | tf_op jit(solution)/shard_map/while/body/eval_jaxpr/jit(_take)/gather | solution.py:11
  132.3 6.5 %select_reduce_fusion.2 = f32[8,32,32]{2,1,0:T(8,128)S(1)} fusion(pred[72]{0:T(512)(128)(4,1)S(1)} %iota_compare_fusion.3, bf16[8,32,72,128]{3,2,1,0:T(8,128)(2,1)} %bitcast.43, pred[8,32]{1,0:T(8,128)(4,1)S(1)} %compare_and_fusion.2, bf16[16,8,32,128]{3,2,1,0:T(8,128)(2,1)} %get-tuple-element.92, s32[]{:T(128)} %get-tuple-element.81), kind=kOutput, calls=%fused_computation.4.clone.1 | convolution fusion | flops 154525696 | bytes 4817736 | tf_op jit(solution)/shard_map/while/body/eval_jaxpr/ntd,ncpd->nctp/dot_general | solution.py:12
  139.0 5.7 %gather_fusion = bf16[256,72,128]{2,1,0:T(8,128)(2,1)} fusion(bf16[256,72,128]{2,1,0:T(8,128)(2,1)} %get-tuple-element.91, s32[1024]{0:T(1024)S(1)} %pad_clamp_fusion.2), kind=kCustom, calls=%fused_computation.clone.1 | custom fusion | bytes 9438208 | tf_op jit(solution)/shard_map/while/body/eval_jaxpr/jit(_take)/gather | solution.py:11
  144.7 6.5 %select_reduce_fusion.2 = f32[8,32,32]{2,1,0:T(8,128)S(1)} fusion(pred[72]{0:T(512)(128)(4,1)S(1)} %iota_compare_fusion.3, bf16[8,32,72,128]{3,2,1,0:T(8,128)(2,1)} %bitcast.43, pred[8,32]{1,0:T(8,128)(4,1)S(1)} %compare_and_fusion.2, bf16[16,8,32,128]{3,2,1,0:T(8,128)(2,1)} %get-tuple-element.92, s32[]{:T(128)} %get-tuple-element.81), kind=kOutput, calls=%fused_computation.4.clone.1 | convolution fusion | flops 154525696 | bytes 4817736 | tf_op jit(solution)/shard_map/while/body/eval_jaxpr/ntd,ncpd->nctp/dot_general | solution.py:12
  151.5 5.7 %gather_fusion = bf16[256,72,128]{2,1,0:T(8,128)(2,1)} fusion(bf16[256,72,128]{2,1,0:T(8,128)(2,1)} %get-tuple-element.91, s32[1024]{0:T(1024)S(1)} %pad_clamp_fusion.2), kind=kCustom, calls=%fused_computation.clone.1 | custom fusion | bytes 9438208 | tf_op jit(solution)/shard_map/while/body/eval_jaxpr/jit(_take)/gather | solution.py:11
  157.2 6.5 %select_reduce_fusion.2 = f32[8,32,32]{2,1,0:T(8,128)S(1)} fusion(pred[72]{0:T(512)(128)(4,1)S(1)} %iota_compare_fusion.3, bf16[8,32,72,128]{3,2,1,0:T(8,128)(2,1)} %bitcast.43, pred[8,32]{1,0:T(8,128)(4,1)S(1)} %compare_and_fusion.2, bf16[16,8,32,128]{3,2,1,0:T(8,128)(2,1)} %get-tuple-element.92, s32[]{:T(128)} %get-tuple-element.81), kind=kOutput, calls=%fused_computation.4.clone.1 | convolution fusion | flops 154525696 | bytes 4817736 | tf_op jit(solution)/shard_map/while/body/eval_jaxpr/ntd,ncpd->nctp/dot_general | solution.py:12
  163.9 5.7 %gather_fusion = bf16[256,72,128]{2,1,0:T(8,128)(2,1)} fusion(bf16[256,72,128]{2,1,0:T(8,128)(2,1)} %get-tuple-element.91, s32[1024]{0:T(1024)S(1)} %pad_clamp_fusion.2), kind=kCustom, calls=%fused_computation.clone.1 | custom fusion | bytes 9438208 | tf_op jit(solution)/shard_map/while/body/eval_jaxpr/jit(_take)/gather | solution.py:11
  169.6 6.5 %select_reduce_fusion.2 = f32[8,32,32]{2,1,0:T(8,128)S(1)} fusion(pred[72]{0:T(512)(128)(4,1)S(1)} %iota_compare_fusion.3, bf16[8,32,72,128]{3,2,1,0:T(8,128)(2,1)} %bitcast.43, pred[8,32]{1,0:T(8,128)(4,1)S(1)} %compare_and_fusion.2, bf16[16,8,32,128]{3,2,1,0:T(8,128)(2,1)} %get-tuple-element.92, s32[]{:T(128)} %get-tuple-element.81), kind=kOutput, calls=%fused_computation.4.clone.1 | convolution fusion | flops 154525696 | bytes 4817736 | tf_op jit(solution)/shard_map/while/body/eval_jaxpr/ntd,ncpd->nctp/dot_general | solution.py:12
  176.4 5.7 %gather_fusion = bf16[256,72,128]{2,1,0:T(8,128)(2,1)} fusion(bf16[256,72,128]{2,1,0:T(8,128)(2,1)} %get-tuple-element.91, s32[1024]{0:T(1024)S(1)} %pad_clamp_fusion.2), kind=kCustom, calls=%fused_computation.clone.1 | custom fusion | bytes 9438208 | tf_op jit(solution)/shard_map/while/body/eval_jaxpr/jit(_take)/gather | solution.py:11
  182.1 6.5 %select_reduce_fusion.2 = f32[8,32,32]{2,1,0:T(8,128)S(1)} fusion(pred[72]{0:T(512)(128)(4,1)S(1)} %iota_compare_fusion.3, bf16[8,32,72,128]{3,2,1,0:T(8,128)(2,1)} %bitcast.43, pred[8,32]{1,0:T(8,128)(4,1)S(1)} %compare_and_fusion.2, bf16[16,8,32,128]{3,2,1,0:T(8,128)(2,1)} %get-tuple-element.92, s32[]{:T(128)} %get-tuple-element.81), kind=kOutput, calls=%fused_computation.4.clone.1 | convolution fusion | flops 154525696 | bytes 4817736 | tf_op jit(solution)/shard_map/while/body/eval_jaxpr/ntd,ncpd->nctp/dot_general | solution.py:12
  188.8 5.7 %gather_fusion = bf16[256,72,128]{2,1,0:T(8,128)(2,1)} fusion(bf16[256,72,128]{2,1,0:T(8,128)(2,1)} %get-tuple-element.91, s32[1024]{0:T(1024)S(1)} %pad_clamp_fusion.2), kind=kCustom, calls=%fused_computation.clone.1 | custom fusion | bytes 9438208 | tf_op jit(solution)/shard_map/while/body/eval_jaxpr/jit(_take)/gather | solution.py:11
  194.5 6.5 %select_reduce_fusion.2 = f32[8,32,32]{2,1,0:T(8,128)S(1)} fusion(pred[72]{0:T(512)(128)(4,1)S(1)} %iota_compare_fusion.3, bf16[8,32,72,128]{3,2,1,0:T(8,128)(2,1)} %bitcast.43, pred[8,32]{1,0:T(8,128)(4,1)S(1)} %compare_and_fusion.2, bf16[16,8,32,128]{3,2,1,0:T(8,128)(2,1)} %get-tuple-element.92, s32[]{:T(128)} %get-tuple-element.81), kind=kOutput, calls=%fused_computation.4.clone.1 | convolution fusion | flops 154525696 | bytes 4817736 | tf_op jit(solution)/shard_map/while/body/eval_jaxpr/ntd,ncpd->nctp/dot_general | solution.py:12
  201.3 5.7 %gather_fusion = bf16[256,72,128]{2,1,0:T(8,128)(2,1)} fusion(bf16[256,72,128]{2,1,0:T(8,128)(2,1)} %get-tuple-element.91, s32[1024]{0:T(1024)S(1)} %pad_clamp_fusion.2), kind=kCustom, calls=%fused_computation.clone.1 | custom fusion | bytes 9438208 | tf_op jit(solution)/shard_map/while/body/eval_jaxpr/jit(_take)/gather | solution.py:11
  207.0 6.5 %select_reduce_fusion.2 = f32[8,32,32]{2,1,0:T(8,128)S(1)} fusion(pred[72]{0:T(512)(128)(4,1)S(1)} %iota_compare_fusion.3, bf16[8,32,72,128]{3,2,1,0:T(8,128)(2,1)} %bitcast.43, pred[8,32]{1,0:T(8,128)(4,1)S(1)} %compare_and_fusion.2, bf16[16,8,32,128]{3,2,1,0:T(8,128)(2,1)} %get-tuple-element.92, s32[]{:T(128)} %get-tuple-element.81), kind=kOutput, calls=%fused_computation.4.clone.1 | convolution fusion | flops 154525696 | bytes 4817736 | tf_op jit(solution)/shard_map/while/body/eval_jaxpr/ntd,ncpd->nctp/dot_general | solution.py:12
  213.7 5.7 %gather_fusion = bf16[256,72,128]{2,1,0:T(8,128)(2,1)} fusion(bf16[256,72,128]{2,1,0:T(8,128)(2,1)} %get-tuple-element.91, s32[1024]{0:T(1024)S(1)} %pad_clamp_fusion.2), kind=kCustom, calls=%fused_computation.clone.1 | custom fusion | bytes 9438208 | tf_op jit(solution)/shard_map/while/body/eval_jaxpr/jit(_take)/gather | solution.py:11
  219.4 6.5 %select_reduce_fusion.2 = f32[8,32,32]{2,1,0:T(8,128)S(1)} fusion(pred[72]{0:T(512)(128)(4,1)S(1)} %iota_compare_fusion.3, bf16[8,32,72,128]{3,2,1,0:T(8,128)(2,1)} %bitcast.43, pred[8,32]{1,0:T(8,128)(4,1)S(1)} %compare_and_fusion.2, bf16[16,8,32,128]{3,2,1,0:T(8,128)(2,1)} %get-tuple-element.92, s32[]{:T(128)} %get-tuple-element.81), kind=kOutput, calls=%fused_computation.4.clone.1 | convolution fusion | flops 154525696 | bytes 4817736 | tf_op jit(solution)/shard_map/while/body/eval_jaxpr/ntd,ncpd->nctp/dot_general | solution.py:12
  226.2 5.7 %gather_fusion = bf16[256,72,128]{2,1,0:T(8,128)(2,1)} fusion(bf16[256,72,128]{2,1,0:T(8,128)(2,1)} %get-tuple-element.91, s32[1024]{0:T(1024)S(1)} %pad_clamp_fusion.2), kind=kCustom, calls=%fused_computation.clone.1 | custom fusion | bytes 9438208 | tf_op jit(solution)/shard_map/while/body/eval_jaxpr/jit(_take)/gather | solution.py:11
  231.9 6.5 %select_reduce_fusion.2 = f32[8,32,32]{2,1,0:T(8,128)S(1)} fusion(pred[72]{0:T(512)(128)(4,1)S(1)} %iota_compare_fusion.3, bf16[8,32,72,128]{3,2,1,0:T(8,128)(2,1)} %bitcast.43, pred[8,32]{1,0:T(8,128)(4,1)S(1)} %compare_and_fusion.2, bf16[16,8,32,128]{3,2,1,0:T(8,128)(2,1)} %get-tuple-element.92, s32[]{:T(128)} %get-tuple-element.81), kind=kOutput, calls=%fused_computation.4.clone.1 | convolution fusion | flops 154525696 | bytes 4817736 | tf_op jit(solution)/shard_map/while/body/eval_jaxpr/ntd,ncpd->nctp/dot_general | solution.py:12
  238.6 5.7 %gather_fusion = bf16[256,72,128]{2,1,0:T(8,128)(2,1)} fusion(bf16[256,72,128]{2,1,0:T(8,128)(2,1)} %get-tuple-element.91, s32[1024]{0:T(1024)S(1)} %pad_clamp_fusion.2), kind=kCustom, calls=%fused_computation.clone.1 | custom fusion | bytes 9438208 | tf_op jit(solution)/shard_map/while/body/eval_jaxpr/jit(_take)/gather | solution.py:11
  244.3 6.5 %select_reduce_fusion.2 = f32[8,32,32]{2,1,0:T(8,128)S(1)} fusion(pred[72]{0:T(512)(128)(4,1)S(1)} %iota_compare_fusion.3, bf16[8,32,72,128]{3,2,1,0:T(8,128)(2,1)} %bitcast.43, pred[8,32]{1,0:T(8,128)(4,1)S(1)} %compare_and_fusion.2, bf16[16,8,32,128]{3,2,1,0:T(8,128)(2,1)} %get-tuple-element.92, s32[]{:T(128)} %get-tuple-element.81), kind=kOutput, calls=%fused_computation.4.clone.1 | convolution fusion | flops 154525696 | bytes 4817736 | tf_op jit(solution)/shard_map/while/body/eval_jaxpr/ntd,ncpd->nctp/dot_general | solution.py:12
  251.1 5.7 %gather_fusion = bf16[256,72,128]{2,1,0:T(8,128)(2,1)} fusion(bf16[256,72,128]{2,1,0:T(8,128)(2,1)} %get-tuple-element.91, s32[1024]{0:T(1024)S(1)} %pad_clamp_fusion.2), kind=kCustom, calls=%fused_computation.clone.1 | custom fusion | bytes 9438208 | tf_op jit(solution)/shard_map/while/body/eval_jaxpr/jit(_take)/gather | solution.py:11
  256.8 6.5 %select_reduce_fusion.2 = f32[8,32,32]{2,1,0:T(8,128)S(1)} fusion(pred[72]{0:T(512)(128)(4,1)S(1)} %iota_compare_fusion.3, bf16[8,32,72,128]{3,2,1,0:T(8,128)(2,1)} %bitcast.43, pred[8,32]{1,0:T(8,128)(4,1)S(1)} %compare_and_fusion.2, bf16[16,8,32,128]{3,2,1,0:T(8,128)(2,1)} %get-tuple-element.92, s32[]{:T(128)} %get-tuple-element.81), kind=kOutput, calls=%fused_computation.4.clone.1 | convolution fusion | flops 154525696 | bytes 4817736 | tf_op jit(solution)/shard_map/while/body/eval_jaxpr/ntd,ncpd->nctp/dot_general | solution.py:12
  263.5 5.7 %gather_fusion = bf16[256,72,128]{2,1,0:T(8,128)(2,1)} fusion(bf16[256,72,128]{2,1,0:T(8,128)(2,1)} %get-tuple-element.91, s32[1024]{0:T(1024)S(1)} %pad_clamp_fusion.2), kind=kCustom, calls=%fused_computation.clone.1 | custom fusion | bytes 9438208 | tf_op jit(solution)/shard_map/while/body/eval_jaxpr/jit(_take)/gather | solution.py:11
  269.2 6.5 %select_reduce_fusion.2 = f32[8,32,32]{2,1,0:T(8,128)S(1)} fusion(pred[72]{0:T(512)(128)(4,1)S(1)} %iota_compare_fusion.3, bf16[8,32,72,128]{3,2,1,0:T(8,128)(2,1)} %bitcast.43, pred[8,32]{1,0:T(8,128)(4,1)S(1)} %compare_and_fusion.2, bf16[16,8,32,128]{3,2,1,0:T(8,128)(2,1)} %get-tuple-element.92, s32[]{:T(128)} %get-tuple-element.81), kind=kOutput, calls=%fused_computation.4.clone.1 | convolution fusion | flops 154525696 | bytes 4817736 | tf_op jit(solution)/shard_map/while/body/eval_jaxpr/ntd,ncpd->nctp/dot_general | solution.py:12
  276.0 5.7 %gather_fusion = bf16[256,72,128]{2,1,0:T(8,128)(2,1)} fusion(bf16[256,72,128]{2,1,0:T(8,128)(2,1)} %get-tuple-element.91, s32[1024]{0:T(1024)S(1)} %pad_clamp_fusion.2), kind=kCustom, calls=%fused_computation.clone.1 | custom fusion | bytes 9438208 | tf_op jit(solution)/shard_map/while/body/eval_jaxpr/jit(_take)/gather | solution.py:11
  281.7 6.5 %select_reduce_fusion.2 = f32[8,32,32]{2,1,0:T(8,128)S(1)} fusion(pred[72]{0:T(512)(128)(4,1)S(1)} %iota_compare_fusion.3, bf16[8,32,72,128]{3,2,1,0:T(8,128)(2,1)} %bitcast.43, pred[8,32]{1,0:T(8,128)(4,1)S(1)} %compare_and_fusion.2, bf16[16,8,32,128]{3,2,1,0:T(8,128)(2,1)} %get-tuple-element.92, s32[]{:T(128)} %get-tuple-element.81), kind=kOutput, calls=%fused_computation.4.clone.1 | convolution fusion | flops 154525696 | bytes 4817736 | tf_op jit(solution)/shard_map/while/body/eval_jaxpr/ntd,ncpd->nctp/dot_general | solution.py:12
  288.3 0.6 broadcast.55
  288.9 0.8 reduce.2
  289.8 0.7 reshape.65
  290.5 6.2 %all-to-all-start.1 = ((f32[32,1,128]{2,1,0:T(1,128)}), f32[32,1,128]{2,1,0:T(1,128)S(1)}, u32[]{:S(2)}, u32[]{:S(2)}) async-start(f32[32,1,128]{2,1,0:T(1,128)} %reshape.65), calls=%async_computation.1 | async-start | bytes 32768 | tf_op jit(solution)/shard_map/all_to_all | solution.py:40
  296.8 9.6 %all-to-all-done.1 = f32[32,1,128]{2,1,0:T(1,128)S(1)} async-done(((f32[32,1,128]{2,1,0:T(1,128)}), f32[32,1,128]{2,1,0:T(1,128)S(1)}, u32[]{:S(2)}, u32[]{:S(2)}) %all-to-all-start.1) | async-done | bytes 16416 | tf_op jit(solution)/shard_map/all_to_all | solution.py:40
  306.3 0.7 reduce.3
  307.3 0.6 copy.14
  (120 shorter events, 3.9 us)
Async XLA Ops:
  6.5 82.6 %all-gather.2.cloned.1.call-start = ((), (), s32[]{:S(2)}) async-start(), calls=%async_computation.2 | async-start | bytes 1081344 | tf_op jit(solution)/shard_map/all_gather | solution.py:34
  8.9 21.2 %all-to-all-start = ((s32[32,1,128]{2,1,0:T(1,128)}), s32[32,1,128]{2,1,0:T(1,128)S(1)}, u32[]{:S(2)}, u32[]{:S(2)}) async-start(s32[32,1,128]{2,1,0:T(1,128)} %reshape.63), calls=%async_computation | async-start | bytes 32768 | tf_op jit(solution)/shard_map/all_to_all | solution.py:36
  89.1 207.6 %copy-start = (s32[4,32]{1,0:T(4,128)S(1)}, s32[4,32]{1,0:T(4,128)}, u32[]{:S(2)}) copy-start(s32[4,32]{1,0:T(4,128)} %param.9) | copy-start | bytes 1540
  290.5 15.9 %all-to-all-start.1 = ((f32[32,1,128]{2,1,0:T(1,128)}), f32[32,1,128]{2,1,0:T(1,128)S(1)}, u32[]{:S(2)}, u32[]{:S(2)}) async-start(f32[32,1,128]{2,1,0:T(1,128)} %reshape.65), calls=%async_computation.1 | async-start | bytes 32768 | tf_op jit(solution)/shard_map/all_to_all | solution.py:40
Sparse Core Ops, SparseCore 0:
  9.9 79.1 all-gather.1
where the time goes:
time: 316 us; the launch traced here: 315 us
  matrix products  104 us (33%)
  local copies, waits for them, and re-layouts  96.7 us (31%)
  waiting for transfers between devices  77.7 us (25%)
  starting transfers between devices  17.7 us (6%)
  between operations  13.5 us (4%)
  other arithmetic  4.62 us (1%)
    dot_general x16, matrix products, score_group(): jnp.einsum('ntd,ncpd->nctp', query_grp, picked, preferred_element_type=jn...  104 us
    gather x16, local copies, waits for them, and re-layouts, score_group(): picked = jnp.take(passages, row_grp, axis=0)  91.1 us
    all_gather x1, waiting for transfers between devices, body(): everyone = lax.all_gather(queries, 'shard', axis=0, tiled=True)  57.8 us
    all_to_all x1, starting transfers between devices, body(): lax.all_to_all(cand_rows, 'shard', split_axis=1, concat_axis=0, tiled=True)  11.5 us
    all_to_all x1, waiting for transfers between devices, body(): lax.all_to_all(cand_rows, 'shard', split_axis=1, concat_axis=0, tiled=True)  9.65 us
    all_to_all x1, waiting for transfers between devices, body(): lax.all_to_all(values[:, None, :], 'shard', split_axis=0, concat_axis=1,...  9.56 us
  transfers between devices with their start and end apart: 3, of which 3 were waited for; matrix products, arithmetic and copies ran while one was open for 1% of the time, Pallas kernels for 0%

commit v1 on v0

v1 whole, which is shorter than its diff:
```python
import functools

import jax
import jax.numpy as jnp
from jax import lax
from jax.experimental import pallas as pl
from jax.experimental.pallas import tpu as pltpu
from jax.sharding import PartitionSpec as P

PLEN = 70
PTOK = 72
NZ = 8
NY = 4
N = NZ * NY
CAP = 32
QTOK = 32
GROUP = 16
Y_ORDER = (0, 1, 3, 2)
MESH = pl.DeviceIdType.MESH


def partner(me, i, dy, sign):
    dz = ((i + 1) // 2) * (2 * (i % 2) - 1)
    z, y = me // NY, me % NY
    return ((z + sign * dz + NZ) % NZ) * NY + (y + sign * dy + NY) % NY


def score_block(query_block, rows, block, passages):
    token = lax.broadcasted_iota(jnp.int32, (8, 128), 0)
    best = []
    for first in range(0, 128, GROUP):
        picked = [passages[rows[block, 0, first + k] & 255] for k in range(GROUP)]
        sims = lax.dot_general(
            jnp.concatenate(picked, 0), query_block, (((1,), (1,)), ((), ())), preferred_element_type=jnp.float32
        ).reshape(GROUP, PTOK // 8, 8, 128)
        head = jnp.max(sims[:, : PTOK // 8 - 1], axis=1)
        tail = jnp.where(token[None] < PLEN - (PTOK - 8), sims[:, PTOK // 8 - 1], -jnp.inf)
        best.append(jnp.max(jnp.maximum(head, tail), axis=1))
    best = jnp.concatenate(best, 0)
    slot = lax.broadcasted_iota(jnp.int32, (128, 128), 0)
    lane = lax.broadcasted_iota(jnp.int32, (128, 128), 1)
    own = jnp.where(slot // CAP == lane // QTOK, best, 0.0)
    mean = jnp.sum(own, axis=1, keepdims=True) * (1.0 / QTOK)
    return jnp.sum(jnp.where(slot == lane, mean, 0.0), axis=0, keepdims=True)


def kernel(queries, passages, cand_rows, cand_counts, out, held, corpus, rows_out, rows_in, rows_s, score_out, score_in,
           load_sem, q_send, q_recv, r_send, r_recv, s_send, s_recv, own_sem):
    me = lax.axis_index("shard")

    def q_copy(k, to, slot):
        return pltpu.make_async_remote_copy(
            src_ref=queries, dst_ref=held.at[slot], send_sem=q_send.at[k], recv_sem=q_recv.at[k],
            device_id={"shard": to}, device_id_type=MESH)

    def r_copy(k, to):
        return pltpu.make_async_remote_copy(
            src_ref=rows_out.at[to], dst_ref=rows_in.at[k], send_sem=r_send.at[k], recv_sem=r_recv.at[k],
            device_id={"shard": to}, device_id_type=MESH)

    def s_copy(k, to):
        return pltpu.make_async_remote_copy(
            src_ref=score_out.at[k], dst_ref=score_in.at[me], send_sem=s_send.at[k], recv_sem=s_recv.at[k],
            device_id={"shard": to}, device_id_type=MESH)

    loads = []
    quarter = passages.shape[0] // 4
    for part in range(4):
        span = pl.ds(part * quarter, quarter)
        loads.append(pltpu.make_async_copy(passages.at[span], corpus.at[span], load_sem.at[part]))
        loads[-1].start()

    barrier = pltpu.get_barrier_semaphore()
    for i in range(NZ):
        for j, dy in enumerate(Y_ORDER):
            if i or j:
                pl.semaphore_signal(barrier, inc=1, device_id={"shard": partner(me, i, dy, 1)}, device_id_type=MESH)
    packed = jnp.concatenate([cand_rows[q] for q in range(4)], axis=1)
    for s in range(N):
        rows_out[s] = packed[s : s + 1]
    own_rows = pltpu.make_async_copy(rows_out.at[me], rows_in.at[0], own_sem.at[0])
    own_rows.start()
    own_queries = pltpu.make_async_copy(queries, held.at[0], own_sem.at[1])
    own_queries.start()
    pl.semaphore_wait(barrier, N - 1)

    for i in range(NZ):
        for j, dy in enumerate(Y_ORDER):
            if i or j:
                r_copy(i * NY + j, partner(me, i, dy, 1)).start()
    for i in range(NZ):
        for j, dy in enumerate(Y_ORDER):
            if i or j:
                k = i * NY + j
                q_copy(k, partner(me, i, dy, 1), k).start()

    own_rows.wait()
    own_queries.wait()
    for k in range(1, N):
        r_copy(k, me).wait_recv()
    to_smem = pltpu.make_async_copy(rows_in, rows_s, own_sem.at[2])
    to_smem.start()
    for load in loads:
        load.wait()
    to_smem.wait()

    def step(i, _):
        for j, dy in enumerate(Y_ORDER):
            k = i * NY + j

            @pl.when(k > 0)
            def _():
                q_copy(k, me, k).wait_recv()

        for j, dy in enumerate(Y_ORDER):
            k = i * NY + j
            score_out[k] = score_block(held[k], rows_s, k, corpus)
        for j, dy in enumerate(Y_ORDER):
            k = i * NY + j

            @pl.when(k > 0)
            def _():
                s_copy(k, partner(me, i, dy, -1)).start()

        return 0

    lax.fori_loop(0, NZ, step, 0)
    own_score = pltpu.make_async_copy(score_out.at[0], score_in.at[me], own_sem.at[3])
    own_score.start()
    own_score.wait()
    for k in range(1, N):
        q_copy(k, me, k).wait_send()
        r_copy(k, me).wait_send()
        s_copy(k, me).wait_send()
        s_copy(k, me).wait_recv()
    returned = score_in[...].reshape(N, 128)
    slot = lax.broadcasted_iota(jnp.int32, (N, CAP), 1)
    for q in range(4):
        live = slot < cand_counts[q : q + 1, :].reshape(N, 1)
        out[q] = jnp.where(live, returned[:, q * CAP : (q + 1) * CAP], 0.0)


def body(queries, passages, cand_rows, cand_counts):
    count = queries.shape[0]
    block = queries.reshape(count * QTOK, queries.shape[2])
    vmem = pl.BlockSpec(memory_space=pltpu.VMEM)
    dma = pltpu.SemaphoreType.DMA
    return pl.pallas_call(
        kernel,
        out_shape=jax.ShapeDtypeStruct((count, N, CAP), jnp.float32),
        in_specs=[vmem, pl.BlockSpec(memory_space=pl.ANY), vmem, vmem],
        out_specs=vmem,
        scratch_shapes=[
            pltpu.VMEM((N,) + block.shape, jnp.bfloat16),
            pltpu.VMEM(passages.shape, jnp.bfloat16),
            pltpu.VMEM((N, 1, 128), jnp.int32),
            pltpu.VMEM((N, 1, 128), jnp.int32),
            pltpu.SMEM((N, 1, 128), jnp.int32),
            pltpu.VMEM((N, 1, 128), jnp.float32),
            pltpu.VMEM((N, 1, 128), jnp.float32),
            dma((4,)),
            dma((N,)), dma((N,)), dma((N,)), dma((N,)), dma((N,)), dma((N,)),
            dma((4,)),
        ],
        compiler_params=pltpu.CompilerParams(collective_id=0, has_side_effects=True, vmem_limit_bytes=32 << 20),
        cost_estimate=pl.CostEstimate(flops=2 * 4096 * 72 * 32 * 128, bytes_accessed=6 << 20, transcendentals=0),
        name="maxsim",
    )(block, passages, cand_rows, cand_counts)


def solution(mesh):
    return jax.shard_map(
        body,
        mesh=mesh,
        in_specs=(
            P(("shard", "rep"), None, None),
            P("shard", None, None),
            P(("shard", "rep"), None, None),
            P(("shard", "rep"), None),
        ),
        out_specs=P(("shard", "rep"), None, None),
        check_vma=False,
    )
```

time: 316 us -> 55.5 us (0.18)
  matrix products: 104 us -> 0 us
  local copies, waits for them, and re-layouts: 96.7 us -> 5.25 us
  waiting for transfers between devices: 77.7 us -> 0 us
  Pallas kernels: 0 us -> 50 us
  starting transfers between devices: 17.7 us -> 0 us
  between operations: 13.5 us -> 0.01 us
  other arithmetic: 4.62 us -> 0 us
    dot_general x16 -> x0, matrix products: 104 us -> none  [score_group(): jnp.einsum('ntd,ncpd->nctp', query_grp, picked, preferred_element_type=jn...]
    gather x16 -> x0, local copies, waits for them, and re-layouts: 91.1 us -> none  [score_group(): picked = jnp.take(passages, row_grp, axis=0)]
    all_gather x1 -> x0, waiting for transfers between devices: 57.8 us -> none  [body(): everyone = lax.all_gather(queries, 'shard', axis=0, tiled=True)]
    pallas_call x0 -> x1, Pallas kernels: none -> 50 us  [body(): pl.pallas_call(kernel, out_shape=jax.ShapeDtypeStruct((count, N, CAP), jn...]
    all_to_all x2 -> x0, waiting for transfers between devices: 19.2 us -> none  [the longest x1 9.65 us: body(): lax.all_to_all(cand_rows, 'shard', split_axis=1, concat_axis=0, tiled=True)]
    all_to_all x2 -> x0, starting transfers between devices: 17.7 us -> none  [the longest x1 11.5 us: body(): lax.all_to_all(cand_rows, 'shard', split_axis=1, concat_axis=0, tiled=True)]
  transfers between devices with their start and end apart: 3 -> 0, of which waited for: 3 -> 0; matrix products, arithmetic and copies ran while one was open for 1% -> 0% of each run, Pallas kernels for 0% -> 0%
where the time goes in v1:
time: 55.5 us; the launch traced here: 55.2 us
  Pallas kernels  50 us (90%)
  local copies, waits for them, and re-layouts  5.25 us (9%)
    pallas_call x1, Pallas kernels, body(): pl.pallas_call(kernel, out_shape=jax.ShapeDtypeStruct((count, N, CAP), jn...  50 us
    unnamed x9, local copies, waits for them, and re-layouts  5.25 us

profile of v1, /device:TPU:4, one launch (start us, length us, event | category | flops | bytes accessed | tf_op | source)
XLA Modules:
  0.0 55.2 jit_solution(4807524627807192967)
XLA Ops:
  0.0 0.0 copy-start
  0.0 2.3 %copy-done = bf16[256,72,128]{2,1,0:T(8,128)(2,1)S(1)} copy-done((bf16[256,72,128]{2,1,0:T(8,128)(2,1)S(1)}, bf16[256,72,128]{2,1,0:T(8,128)(2,1)}, u32[]{:S(2)}) %copy-start) | copy-done | bytes 4718616
  2.3 0.0 copy-start.1
  2.3 0.8 %copy-done.1 = s32[4,32,32]{2,1,0:T(8,128)S(1)} copy-done((s32[4,32,32]{2,1,0:T(8,128)S(1)}, s32[4,32,32]{2,1,0:T(8,128)}, u32[]{:S(2)}) %copy-start.1) | copy-done | bytes 16408
  3.2 0.0 copy-start.2
  3.2 0.8 %copy-done.2 = bf16[4,32,128]{2,1,0:T(8,128)(2,1)S(1)} copy-done((bf16[4,32,128]{2,1,0:T(8,128)(2,1)S(1)}, bf16[4,32,128]{2,1,0:T(8,128)(2,1)}, u32[]{:S(2)}) %copy-start.2) | copy-done | bytes 32792
  3.9 0.0 copy-start.3
  3.9 0.7 %copy-done.3 = s32[4,32]{1,0:T(4,128)S(1)} copy-done((s32[4,32]{1,0:T(4,128)S(1)}, s32[4,32]{1,0:T(4,128)}, u32[]{:S(2)}) %copy-start.3) | copy-done | bytes 536
  4.6 50.0 %maxsim.1 = f32[4,32,32]{2,1,0:T(8,128)S(1)} custom-call(bf16[128,128]{1,0:T(8,128)(2,1)S(1)} %bitcast.1, bf16[256,72,128]{2,1,0:T(8,128)(2,1)S(1)} %copy-done, s32[4,32,32]{2,1,0:T(8,128)S(1)} %copy-done.1, s32[4,32]{1,0:T(4,128)S(1)} %copy-done.3), custom_call_target="tpu_custom_call" | custom-call | flops 2415919104 | bytes 6291456 | tf_op jit(solution)/shard_map/maxsim/pallas_call | solution.py:148
  54.6 0.6 %copy.6 = f32[4,32,32]{2,1,0:T(8,128)} copy(f32[4,32,32]{2,1,0:T(8,128)S(1)} %maxsim.1) | data formatting | bytes 32768
Async XLA Ops:
  0.0 2.3 %copy-start = (bf16[256,72,128]{2,1,0:T(8,128)(2,1)S(1)}, bf16[256,72,128]{2,1,0:T(8,128)(2,1)}, u32[]{:S(2)}) copy-start(bf16[256,72,128]{2,1,0:T(8,128)(2,1)} %passages.1) | copy-start | bytes 14155780
  2.3 0.8 %copy-start.1 = (s32[4,32,32]{2,1,0:T(8,128)S(1)}, s32[4,32,32]{2,1,0:T(8,128)}, u32[]{:S(2)}) copy-start(s32[4,32,32]{2,1,0:T(8,128)} %cand_rows.1) | copy-start | bytes 49156
  3.2 0.8 %copy-start.2 = (bf16[4,32,128]{2,1,0:T(8,128)(2,1)S(1)}, bf16[4,32,128]{2,1,0:T(8,128)(2,1)}, u32[]{:S(2)}) copy-start(bf16[4,32,128]{2,1,0:T(8,128)(2,1)} %param.4) | copy-start | bytes 98308
  3.9 0.7 %copy-start.3 = (s32[4,32]{1,0:T(4,128)S(1)}, s32[4,32]{1,0:T(4,128)}, u32[]{:S(2)}) copy-start(s32[4,32]{1,0:T(4,128)} %cand_counts.1) | copy-start | bytes 1540

commit v2 on v0

v2 whole, which is shorter than its diff:
```python
import jax
import jax.numpy as jnp
from jax import lax
from jax.experimental import pallas as pl
from jax.experimental.pallas import tpu as pltpu
from jax.sharding import PartitionSpec as P

PLEN = 70
PTOK = 72
NZ = 8
NY = 4
HALF = NZ // 2
N = NZ * NY
CAP = 32
QTOK = 32
LANES = 128
GROUP = 16
MESH = pl.DeviceIdType.MESH


def plane(i, z):
    near = (z + i) % HALF
    if_low = jnp.where(i < HALF, near, HALF + near)
    if_high = jnp.where((i < 2) | (i >= 2 + HALF), HALF + near, i - 2)
    return jnp.where(z < HALF, if_low, if_high)


def score_block(query_block, row_at, passages):
    token = lax.broadcasted_iota(jnp.int32, (8, LANES), 0)
    best = []
    for first in range(0, LANES, GROUP):
        picked = [passages[row_at(first + k) & 255] for k in range(GROUP)]
        sims = lax.dot_general(
            jnp.concatenate(picked, 0), query_block, (((1,), (1,)), ((), ())), preferred_element_type=jnp.float32
        ).reshape(GROUP, PTOK // 8, 8, LANES)
        head = jnp.max(sims[:, : PTOK // 8 - 1], axis=1)
        tail = jnp.where(token[None] < PLEN - (PTOK - 8), sims[:, PTOK // 8 - 1], -jnp.inf)
        best.append(jnp.max(jnp.maximum(head, tail), axis=1))
    best = jnp.concatenate(best, 0)
    slot = lax.broadcasted_iota(jnp.int32, (LANES, LANES), 0)
    lane = lax.broadcasted_iota(jnp.int32, (LANES, LANES), 1)
    own = jnp.where(slot // CAP == lane // QTOK, best, 0.0)
    mean = jnp.sum(own, axis=1, keepdims=True) * (1.0 / QTOK)
    return jnp.sum(jnp.where(slot == lane, mean, 0.0), axis=0, keepdims=True)


def kernel(queries, passages, cand_rows, cand_counts, out, held, corpus, rows_v, rows_s, score_out, score_in,
           own_rows, own_counts, load_sem, in_sem, rows_sem, q_send, q_recv, s_send, s_recv, ready_z, ready_y):
    me = lax.axis_index("shard")
    z, y = me // NY, me % NY

    def send_block(s, to):
        pltpu.make_async_remote_copy(
            src_ref=held.at[s], dst_ref=held.at[s], send_sem=q_send, recv_sem=q_recv.at[s],
            device_id={"shard": to}, device_id_type=MESH).start()

    def wait_block(s):
        pltpu.make_async_copy(held.at[s], held.at[s], q_recv.at[s]).wait()

    def send_score(s):
        @pl.when(s != me)
        def _():
            pltpu.make_async_remote_copy(
                src_ref=score_out.at[s], dst_ref=score_in.at[me], send_sem=s_send, recv_sem=s_recv,
                device_id={"shard": s}, device_id_type=MESH).start()

    def spread(i):
        s = plane(i, z) * NY + y
        wait_block(s)
        for dy in range(1, NY):
            send_block(s, z * NY + (y + dy) % NY)

    def unpack_rows(i):
        mine = lax.broadcasted_iota(jnp.int32, (N, LANES), 0) == me
        for j in range(NY):
            rows = held[plane(i, z) * NY + j, 4 * QTOK :].astype(jnp.float32)
            rows_v[i, j : j + 1] = jnp.sum(jnp.where(mine, rows, 0.0), axis=0, keepdims=True).astype(jnp.int32)
        pltpu.make_async_copy(rows_v.at[i], rows_s.at[i], rows_sem.at[i]).start()

    def collect(i):
        for dy in range(1, NY):
            wait_block(plane(i, z) * NY + (y + dy) % NY)
        unpack_rows(i)

    rows_in = pltpu.make_async_copy(cand_rows, own_rows, in_sem.at[0])
    queries_in = pltpu.make_async_copy(queries, held.at[me, pl.ds(0, 4 * QTOK)], in_sem.at[1])
    counts_in = pltpu.make_async_copy(cand_counts, own_counts, in_sem.at[2])
    rows_in.start()
    queries_in.start()
    counts_in.start()
    loads = []
    part = passages.shape[0] // 4
    for k in range(4):
        span = pl.ds(k * part, part)
        loads.append(pltpu.make_async_copy(passages.at[span], corpus.at[span], load_sem.at[k]))
        loads[-1].start()

    barrier = pltpu.get_barrier_semaphore()
    for d in range(1, NZ):
        to = (z + d) % NZ

        @pl.when(to > z)
        def _():
            pl.semaphore_signal(barrier, inc=1, device_id={"shard": to * NY + y}, device_id_type=MESH)

    for d in range(1, NY):
        to = (y + d) % NY

        @pl.when(to > y)
        def _():
            pl.semaphore_signal(barrier, inc=1, device_id={"shard": z * NY + to}, device_id_type=MESH)

    rows_in.wait()
    packed = jnp.concatenate([own_rows[q] for q in range(4)], axis=1)
    held[me, 4 * QTOK :] = packed.astype(jnp.float32).astype(jnp.bfloat16)
    queries_in.wait()

    @pl.when(me > 0)
    def _():
        pl.semaphore_wait(barrier, z + y)

    for d in range(1, NY):
        to = (y + d) % NY

        @pl.when(to < y)
        def _():
            pl.semaphore_signal(ready_y.at[y], inc=1, device_id={"shard": z * NY + to}, device_id_type=MESH)
            send_block(me, z * NY + to)

    for d in range(1, NZ):
        to = (z + d) % NZ

        @pl.when(to < z)
        def _():
            pl.semaphore_signal(ready_z.at[z], inc=1, device_id={"shard": to * NY + y}, device_id_type=MESH)
            send_block(me, to * NY + y)

    for d in range(1, NY):
        to = y + d

        @pl.when(to < NY)
        def _():
            pl.semaphore_wait(ready_y.at[to], 1)
            send_block(me, z * NY + to)

    def greet_later(first, last):
        for d in range(1, HALF):
            to = z + d

            @pl.when((to >= first) & (to < last))
            def _():
                pl.semaphore_wait(ready_z.at[to], 1)
                send_block(me, to * NY + y)

    greet_later(0, jnp.where(z < HALF, HALF, NZ))
    spread(1)
    collect(0)
    for load in loads:
        load.wait()

    def step(i, _):
        @pl.when((i == 1) & (z < HALF))
        def _():
            for to in range(HALF, NZ):
                pl.semaphore_wait(ready_z.at[to], 1)
                send_block(me, to * NY + y)

        @pl.when(i + 2 < NZ)
        def _():
            spread(i + 2)

        @pl.when(i > 0)
        def _():
            for j in range(NY):
                send_score(plane(i - 1, z) * NY + j)

        @pl.when(i + 1 < NZ)
        def _():
            collect(i + 1)

        pltpu.make_async_copy(rows_v.at[i], rows_s.at[i], rows_sem.at[i]).wait()
        for j in range(NY):
            s = plane(i, z) * NY + j
            score_out[s] = score_block(held[s, : 4 * QTOK], lambda k, j=j: rows_s[i, j, k], corpus)
        return 0

    lax.fori_loop(0, NZ, step, 0)
    for j in range(NY):
        send_score(plane(NZ - 1, z) * NY + j)
    score_in[me] = score_out[me]
    counts_in.wait()
    others = pl.ds(0, N - 1)
    pltpu.make_async_copy(held.at[others], held.at[others], q_send).wait()
    pltpu.make_async_copy(score_in.at[others], score_in.at[others], s_send).wait()
    pltpu.make_async_copy(score_in.at[others], score_in.at[others], s_recv).wait()
    returned = score_in[...].reshape(N, LANES)
    slot = lax.broadcasted_iota(jnp.int32, (N, CAP), 1)
    for q in range(4):
        live = slot < own_counts[q : q + 1, :].reshape(N, 1)
        out[q] = jnp.where(live, returned[:, q * CAP : (q + 1) * CAP], 0.0)


def body(queries, passages, cand_rows, cand_counts):
    count = queries.shape[0]
    block = queries.reshape(count * QTOK, queries.shape[2])
    hbm = pl.BlockSpec(memory_space=pltpu.HBM)
    dma = pltpu.SemaphoreType.DMA
    regular = pltpu.SemaphoreType.REGULAR
    return pl.pallas_call(
        kernel,
        out_shape=jax.ShapeDtypeStruct((count, N, CAP), jnp.float32),
        in_specs=[hbm, hbm, hbm, hbm],
        out_specs=pl.BlockSpec(memory_space=pltpu.VMEM),
        scratch_shapes=[
            pltpu.VMEM((N, block.shape[0] + N, LANES), jnp.bfloat16),
            pltpu.VMEM(passages.shape, jnp.bfloat16),
            pltpu.VMEM((NZ, NY, LANES), jnp.int32),
            pltpu.SMEM((NZ, NY, LANES), jnp.int32),
            pltpu.VMEM((N, 1, LANES), jnp.float32),
            pltpu.VMEM((N, 1, LANES), jnp.float32),
            pltpu.VMEM(cand_rows.shape, jnp.int32),
            pltpu.VMEM(cand_counts.shape, jnp.int32),
            dma((4,)), dma((3,)), dma((NZ,)),
            dma, dma((N,)), dma, dma,
            regular((NZ,)), regular((NY,)),
        ],
        compiler_params=pltpu.CompilerParams(collective_id=0, has_side_effects=True, vmem_limit_bytes=(64 << 20) - (64 << 10)),
        cost_estimate=pl.CostEstimate(flops=2 * 4096 * 72 * 32 * 128, bytes_accessed=6 << 20, transcendentals=0),
        name="maxsim",
    )(block, passages, cand_rows, cand_counts)


def solution(mesh):
    return jax.shard_map(
        body,
        mesh=mesh,
        in_specs=(
            P(("shard", "rep"), None, None),
            P("shard", None, None),
            P(("shard", "rep"), None, None),
            P(("shard", "rep"), None),
        ),
        out_specs=P(("shard", "rep"), None, None),
        check_vma=False,
    )
```

time: 316 us -> 52.3 us (0.17)
  the two profiles are of different devices: /device:TPU:4 before, /device:TPU:192 now
where the time goes in v2:
time: 52.3 us; the launch traced here: 52.2 us
  Pallas kernels  50.7 us (97%)
  local copies, waits for them, and re-layouts  1.47 us (3%)
    pallas_call x1, Pallas kernels, body(): pl.pallas_call(kernel, out_shape=jax.ShapeDtypeStruct((count, N, CAP), jn...  50.7 us
    unnamed x1, local copies, waits for them, and re-layouts  1.47 us

profile of v2, /device:TPU:192, one launch (start us, length us, event | category | flops | bytes accessed | tf_op | source)
XLA Modules:
  0.0 52.2 jit_solution(4669417275312880385)
XLA Ops:
  0.0 50.7 %maxsim.1 = f32[4,32,32]{2,1,0:T(8,128)} custom-call(bf16[128,128]{1,0:T(8,128)(2,1)} %bitcast.1, bf16[256,72,128]{2,1,0:T(8,128)(2,1)} %passages.1, s32[4,32,32]{2,1,0:T(8,128)} %cand_rows.1, s32[4,32]{1,0:T(4,128)} %cand_counts.1), custom_call_target="tpu_custom_call" | custom-call | flops 2415919104 | bytes 6291456 | tf_op jit(solution)/shard_map/maxsim/pallas_call | solution.py:209
  50.8 1.5 %copy.6 = f32[4,32,32]{2,1,0:T(8,128)} copy(f32[4,32,32]{2,1,0:T(8,128)} %maxsim.1) | data formatting | bytes 32768

commit v3 on v2

v3 whole, which is shorter than its diff:
```python
import jax
import jax.numpy as jnp
from jax import lax
from jax.experimental import pallas as pl
from jax.experimental.pallas import tpu as pltpu
from jax.sharding import PartitionSpec as P

PLEN = 70
PTOK = 72
NZ = 8
NY = 4
HALF = NZ // 2
N = NZ * NY
CAP = 32
QTOK = 32
LANES = 128
GROUP = 16
MESH = pl.DeviceIdType.MESH


ORDER = (
    ((0, 0), (0, 3), (1, 3), (0, 2), (1, 2), (0, 1), (1, 0), (1, 1)),
    ((0, 0), (0, 2), (1, 1), (1, 3), (1, 0), (1, 2), (0, 3), (0, 1)),
)
SENDS = (
    {
        -1: (("y", 3), ("o", (0, 3)), ("y", 1), ("y", 2), ("o", (0, 2)), ("o", (1, 3)),),
        0: (("s", 1), ("o", (1, 1)), ("s", 3), ("o", (0, 1)),),
        1: (("o", (1, 2)), ("s", 2), ("o", (1, 0)),),
        2: (("s", 6), ("s", 4),),
        3: (("s", 5),),
        4: (("s", 7),),
    },
    {
        -1: (("y", 3), ("o", (0, 3)), ("y", 1), ("y", 2), ("o", (0, 2)), ("o", (1, 3)),),
        0: (("s", 1), ("o", (1, 1)), ("s", 3), ("o", (0, 1)),),
        1: (("o", (1, 2)), ("s", 2), ("o", (1, 0)),),
        2: (("s", 6), ("s", 4),),
        3: (("s", 5),),
        4: (("s", 7),),
    },
    {
        -1: (("y", 3), ("o", (0, 3)), ("y", 1), ("y", 2), ("o", (0, 2)), ("o", (1, 3)),),
        0: (("s", 1), ("o", (1, 1)), ("s", 3), ("o", (0, 1)),),
        1: (("o", (1, 2)), ("s", 2), ("o", (1, 0)),),
        2: (("s", 6), ("s", 4),),
        3: (("s", 5),),
        4: (("s", 7),),
    },
    {
        -1: (("y", 3), ("o", (0, 3)), ("y", 1), ("y", 2), ("o", (0, 2)), ("o", (1, 3)),),
        0: (("s", 1), ("o", (1, 1)), ("s", 3), ("o", (0, 1)),),
        1: (("o", (1, 2)), ("s", 2), ("o", (1, 0)),),
        2: (("s", 6), ("s", 4),),
        3: (("s", 5),),
        4: (("s", 7),),
    },
    {
        -1: (("y", 1), ("o", (0, 2)), ("y", 3), ("y", 2), ("o", (1, 3)), ("o", (1, 2)), ("s", 1), ("o", (1, 0)),),
        0: (("s", 3),),
        1: (("o", (0, 3)), ("s", 2), ("o", (0, 1)),),
        2: (("o", (1, 1)), ("s", 4), ("s", 5),),
        3: (("s", 6),),
        4: (("s", 7),),
    },
    {
        -1: (("y", 1), ("o", (0, 2)), ("y", 3), ("y", 2), ("o", (1, 3)), ("o", (1, 2)), ("s", 1), ("o", (1, 0)),),
        0: (("s", 3),),
        1: (("o", (0, 3)), ("s", 2), ("o", (0, 1)),),
        2: (("o", (1, 1)), ("s", 4), ("s", 5),),
        3: (("s", 6),),
        4: (("s", 7),),
    },
    {
        -1: (("y", 1), ("o", (0, 2)), ("y", 3), ("y", 2), ("o", (1, 3)), ("o", (1, 2)), ("s", 1), ("o", (1, 0)),),
        0: (("s", 3),),
        1: (("o", (0, 3)), ("s", 2), ("o", (0, 1)),),
        2: (("o", (1, 1)), ("s", 4), ("s", 5),),
        3: (("s", 6),),
        4: (("s", 7),),
    },
    {
        -1: (("y", 1), ("o", (0, 2)), ("y", 3), ("y", 2), ("o", (1, 3)), ("o", (1, 2)), ("s", 1), ("o", (1, 0)),),
        0: (("s", 3),),
        1: (("o", (0, 3)), ("s", 2), ("o", (0, 1)),),
        2: (("o", (1, 1)), ("s", 4), ("s", 5),),
        3: (("s", 6),),
        4: (("s", 7),),
    },
)
ROWS_AT = (
    (-1, 1, 2, 2, 4, 5, 5, 6),
    (-1, 1, 2, 2, 3, 4, 5, 6),
)


def apart(a, b):
    return ((a // 2 + b // 2) % 2) * 2 + (a + b) % 2


def choose(values, i):
    if isinstance(i, int):
        return values[i]
    found = values[0]
    for n, value in enumerate(values[1:], 1):
        found = jnp.where(i == n, value, found)
    return found


def plane(i, z):
    other, k = (
        jnp.where(z < HALF, choose([e[n] for e in ORDER[0]], i), choose([e[n] for e in ORDER[1]], i)) for n in range(2)
    )
    return HALF * ((z // HALF + other) % 2) + apart(z % HALF, k)


def score_block(query_block, row_at, passages):
    token = lax.broadcasted_iota(jnp.int32, (8, LANES), 0)
    best = []
    for first in range(0, LANES, GROUP):
        picked = [passages[row_at(first + k) & 255] for k in range(GROUP)]
        sims = lax.dot_general(
            jnp.concatenate(picked, 0), query_block, (((1,), (1,)), ((), ())), preferred_element_type=jnp.float32
        ).reshape(GROUP, PTOK // 8, 8, LANES)
        head = jnp.max(sims[:, : PTOK // 8 - 1], axis=1)
        tail = jnp.where(token[None] < PLEN - (PTOK - 8), sims[:, PTOK // 8 - 1], -jnp.inf)
        best.append(jnp.max(jnp.maximum(head, tail), axis=1))
    best = jnp.concatenate(best, 0)
    slot = lax.broadcasted_iota(jnp.int32, (LANES, LANES), 0)
    lane = lax.broadcasted_iota(jnp.int32, (LANES, LANES), 1)
    own = jnp.where(slot // CAP == lane // QTOK, best, 0.0)
    mean = jnp.sum(own, axis=1, keepdims=True) * (1.0 / QTOK)
    return jnp.sum(jnp.where(slot == lane, mean, 0.0), axis=0, keepdims=True)


def kernel(queries, passages, cand_rows, out, held, held_rows, own_for, corpus, rows_v, rows_s, score_out,
           score_in, own_rows, load_sem, in_sem, rows_sem, q_send, q_recv, r_send, r_recv, s_send, s_recv,
           ready_z, ready_y):
    me = lax.axis_index("shard")
    z, y = me // NY, me % NY

    def send(rows, s, to):
        for src, ref, send_sem, recv_sem in ((rows, held_rows, r_send, r_recv), (held.at[s], held, q_send, q_recv)):
            pltpu.make_async_remote_copy(
                src_ref=src, dst_ref=ref.at[s], send_sem=send_sem, recv_sem=recv_sem.at[s],
                device_id={"shard": to}, device_id_type=MESH).start()

    def send_own(to):
        send(own_for.at[to // NY], me, to)

    def wait_rows(s):
        pltpu.make_async_copy(held_rows.at[s], held_rows.at[s], r_recv.at[s]).wait()

    def wait_block(s):
        pltpu.make_async_copy(held.at[s], held.at[s], q_recv.at[s]).wait()

    def send_score(s):
        @pl.when(s != me)
        def _():
            pltpu.make_async_remote_copy(
                src_ref=score_out.at[s], dst_ref=score_in.at[me], send_sem=s_send, recv_sem=s_recv,
                device_id={"shard": s}, device_id_type=MESH).start()

    def spread(i):
        s = plane(i, z) * NY + y
        wait_rows(s)
        wait_block(s)
        for dy in (2, 1, 3):
            send(held_rows.at[s], s, z * NY + (y + dy) % NY)

    def unpack_rows(i):
        for dy in range(1, NY):
            wait_rows(plane(i, z) * NY + (y + dy) % NY)
        mine = lax.broadcasted_iota(jnp.int32, (16, LANES), 0) == y
        for j in range(NY):
            rows = held_rows[plane(i, z) * NY + j].astype(jnp.float32)
            rows_v[i, j : j + 1] = jnp.sum(jnp.where(mine, rows, 0.0), axis=0, keepdims=True).astype(jnp.int32)
        pltpu.make_async_copy(rows_v.at[i], rows_s.at[i], rows_sem.at[i]).start()

    rows_in = pltpu.make_async_copy(cand_rows, own_rows, in_sem.at[0])
    queries_in = pltpu.make_async_copy(queries, held.at[me], in_sem.at[1])
    rows_in.start()
    queries_in.start()
    loads = []
    part = passages.shape[0] // 4
    for k in range(4):
        span = pl.ds(k * part, part)
        loads.append(pltpu.make_async_copy(passages.at[span], corpus.at[span], load_sem.at[k]))
        loads[-1].start()

    barrier = pltpu.get_barrier_semaphore()
    for d in range(1, NZ):
        to = (z + d) % NZ

        @pl.when(to > z)
        def _():
            pl.semaphore_signal(barrier, inc=1, device_id={"shard": to * NY + y}, device_id_type=MESH)

    for d in range(1, NY):
        to = (y + d) % NY

        @pl.when(to > y)
        def _():
            pl.semaphore_signal(barrier, inc=1, device_id={"shard": z * NY + to}, device_id_type=MESH)

    rows_in.wait()
    packed = jnp.concatenate([own_rows[q] for q in range(4)], axis=1).astype(jnp.float32)
    for to in range(NZ):
        piece = jnp.concatenate([packed[to * NY : (to + 1) * NY], jnp.zeros((16 - NY, LANES), jnp.float32)], axis=0)
        own_for[to] = piece.astype(jnp.bfloat16)
    held_rows[me] = own_for[z]
    queries_in.wait()

    @pl.when(me > 0)
    def _():
        pl.semaphore_wait(barrier, z + y)

    for to in range(NY):

        @pl.when(to < y)
        def _():
            pl.semaphore_signal(ready_y.at[y], inc=1, device_id={"shard": z * NY + to}, device_id_type=MESH)

    for to in range(NZ):

        @pl.when(to < z)
        def _():
            pl.semaphore_signal(ready_z.at[z], inc=1, device_id={"shard": to * NY + y}, device_id_type=MESH)

    for d in (1, 3, 2):
        to = apart(y, d)

        @pl.when(to < y)
        def _():
            send_own(z * NY + to)

    for k in (1, 2, 3):
        to = z - z % HALF + apart(z % HALF, k)

        @pl.when(to < z)
        def _():
            send_own(to * NY + y)

    def send_y(d):
        to = apart(y, d)

        @pl.when(to > y)
        def _():
            pl.semaphore_wait(ready_y.at[to], 1)
            send_own(z * NY + to)

    def send_z(other, k):
        to = HALF * ((z // HALF + other) % 2) + apart(z % HALF, k)

        @pl.when(to > z)
        def _():
            pl.semaphore_wait(ready_z.at[to], 1)
            send_own(to * NY + y)

        if other:

            @pl.when(to < z)
            def _():
                send_own(to * NY + y)

    def send_at(at, now=True):
        for here in range(NZ):
            if at in SENDS[here]:

                @pl.when((z == here) & now)
                def _(here=here):
                    for kind, what in SENDS[here][at]:
                        if kind == "y":
                            send_y(what)
                        elif kind == "o":
                            send_z(*what)
                        else:
                            spread(what)

    send_at(-1)
    unpack_rows(0)
    for load in loads:
        load.wait()

    def step(i, _):
        for at in range(NZ):
            send_at(at, i == at)

        @pl.when(i > 0)
        def _():
            for j in range(NY):
                send_score(plane(i - 1, z) * NY + j)

        rows_at = jnp.where(z < HALF, choose(ROWS_AT[0], i), choose(ROWS_AT[1], i))
        later = jnp.minimum(i + 1, NZ - 1)
        later_at = jnp.where(z < HALF, choose(ROWS_AT[0], later), choose(ROWS_AT[1], later))

        @pl.when(rows_at == i)
        def _():
            unpack_rows(i)

        @pl.when((i + 1 < NZ) & (later_at == i))
        def _():
            unpack_rows(i + 1)

        for dy in range(1, NY):
            wait_block(plane(i, z) * NY + (y + dy) % NY)
        pltpu.make_async_copy(rows_v.at[i], rows_s.at[i], rows_sem.at[i]).wait()
        for j in range(NY):
            s = plane(i, z) * NY + j
            score_out[s] = score_block(held[s], lambda k, j=j: rows_s[i, j, k], corpus)
        return 0

    lax.fori_loop(0, NZ, step, 0)
    for j in range(NY):
        send_score(plane(NZ - 1, z) * NY + j)
    others = pl.ds(0, N - 1)
    pltpu.make_async_copy(score_in.at[others], score_in.at[others], s_recv).wait()
    score_in[me] = score_out[me]
    returned = score_in[...].reshape(N, LANES)
    for q in range(4):
        out[q] = returned[:, q * CAP : (q + 1) * CAP]
    pltpu.make_async_copy(held.at[others], held.at[others], q_send).wait()
    pltpu.make_async_copy(held_rows.at[others], held_rows.at[others], r_send).wait()
    pltpu.make_async_copy(score_in.at[others], score_in.at[others], s_send).wait()


def body(queries, passages, cand_rows, cand_counts):
    count = queries.shape[0]
    block = queries.reshape(count * QTOK, queries.shape[2])
    hbm = pl.BlockSpec(memory_space=pltpu.HBM)
    dma = pltpu.SemaphoreType.DMA
    regular = pltpu.SemaphoreType.REGULAR
    returned = pl.pallas_call(
        kernel,
        out_shape=jax.ShapeDtypeStruct((count, N, CAP), jnp.float32),
        in_specs=[hbm, hbm, hbm],
        out_specs=pl.BlockSpec(memory_space=pltpu.VMEM),
        scratch_shapes=[
            pltpu.VMEM((N,) + block.shape, jnp.bfloat16),
            pltpu.VMEM((N, 16, LANES), jnp.bfloat16),
            pltpu.VMEM((NZ, 16, LANES), jnp.bfloat16),
            pltpu.VMEM(passages.shape, jnp.bfloat16),
            pltpu.VMEM((NZ, NY, LANES), jnp.int32),
            pltpu.SMEM((NZ, NY, LANES), jnp.int32),
            pltpu.VMEM((N, 1, LANES), jnp.float32),
            pltpu.VMEM((N, 1, LANES), jnp.float32),
            pltpu.VMEM(cand_rows.shape, jnp.int32),
            dma((4,)), dma((2,)), dma((NZ,)),
            dma, dma((N,)), dma, dma((N,)), dma, dma,
            regular((NZ,)), regular((NY,)),
        ],
        compiler_params=pltpu.CompilerParams(collective_id=0, has_side_effects=True, vmem_limit_bytes=(64 << 20) - (64 << 10)),
        cost_estimate=pl.CostEstimate(flops=2 * 4096 * 72 * 32 * 128, bytes_accessed=6 << 20, transcendentals=0),
        name="maxsim",
    )(block, passages, cand_rows)
    live = jnp.arange(CAP)[None, None, :] < cand_counts[:, :, None]
    return jnp.where(live, returned, jnp.float32(0.0))


def solution(mesh):
    return jax.shard_map(
        body,
        mesh=mesh,
        in_specs=(
            P(("shard", "rep"), None, None),
            P("shard", None, None),
            P(("shard", "rep"), None, None),
            P(("shard", "rep"), None),
        ),
        out_specs=P(("shard", "rep"), None, None),
        check_vma=False,
    )
```

time: 52.3 us -> 44.3 us (0.85)
  the two profiles are of different devices: /device:TPU:192 before, /device:TPU:4 now
where the time goes in v3:
time: 44.3 us; the launch traced here: 44.1 us
  Pallas kernels  42.5 us (96%)
  other arithmetic  1.56 us (4%)
    pallas_call x1, Pallas kernels, body(): pl.pallas_call(kernel, out_shape=jax.ShapeDtypeStruct((count, N, CAP), jn...  42.5 us
    select_n x1, other arithmetic, body(): return jnp.where(live, returned, jnp.float32(0.0))  1.56 us

profile of v3, /device:TPU:4, one launch (start us, length us, event | category | flops | bytes accessed | tf_op | source)
XLA Modules:
  0.0 44.1 jit_solution(4276544813189525572)
XLA Ops:
  0.0 42.5 %maxsim.1 = f32[4,32,32]{2,1,0:T(8,128)} custom-call(bf16[128,128]{1,0:T(8,128)(2,1)} %bitcast.1, bf16[256,72,128]{2,1,0:T(8,128)(2,1)} %passages.1, s32[4,32,32]{2,1,0:T(8,128)} %cand_rows.1), custom_call_target="tpu_custom_call" | custom-call | flops 2415919104 | bytes 6291456 | tf_op jit(solution)/shard_map/maxsim/pallas_call | solution.py:334
  42.5 1.6 %fusion = f32[4,32,32]{2,1,0:T(8,128)} fusion(f32[4,32,32]{2,1,0:T(8,128)} %maxsim.1, s32[4,32]{1,0:T(4,128)} %param.7), kind=kLoop, calls=%fused_computation.1 | loop fusion | flops 8192 | bytes 33280 | tf_op jit(solution)/shard_map/jit(_where)/select_n | solution.py:358

commit v4 on v3

--- a/solution.py
+++ b/solution.py
@@ -107,10 +107,9 @@
     return found
 
 
-def plane(i, z):
-    other, k = (
-        jnp.where(z < HALF, choose([e[n] for e in ORDER[0]], i), choose([e[n] for e in ORDER[1]], i)) for n in range(2)
-    )
+def plane(n, z):
+    (low, near), (high, far) = ORDER[0][n], ORDER[1][n]
+    other, k = jnp.where(z < HALF, low, high), jnp.where(z < HALF, near, far)
     return HALF * ((z // HALF + other) % 2) + apart(z % HALF, k)
 
 
@@ -138,6 +137,8 @@
            ready_z, ready_y):
     me = lax.axis_index("shard")
     z, y = me // NY, me % NY
+    bases = [plane(n, z) * NY for n in range(NZ)]
+    others_y = [(y + dy) % NY for dy in range(1, NY)]
 
     def send(rows, s, to):
         for src, ref, send_sem, recv_sem in ((rows, held_rows, r_send, r_recv), (held.at[s], held, q_send, q_recv)):
@@ -162,18 +163,19 @@
                 device_id={"shard": s}, device_id_type=MESH).start()
 
     def spread(i):
-        s = plane(i, z) * NY + y
+        s = bases[i] + y
         wait_rows(s)
         wait_block(s)
         for dy in (2, 1, 3):
-            send(held_rows.at[s], s, z * NY + (y + dy) % NY)
+            send(held_rows.at[s], s, z * NY + others_y[dy - 1])
 
     def unpack_rows(i):
-        for dy in range(1, NY):
-            wait_rows(plane(i, z) * NY + (y + dy) % NY)
+        base = choose(bases, i)
+        for other in others_y:
+            wait_rows(base + other)
         mine = lax.broadcasted_iota(jnp.int32, (16, LANES), 0) == y
         for j in range(NY):
-            rows = held_rows[plane(i, z) * NY + j].astype(jnp.float32)
+            rows = held_rows[base + j].astype(jnp.float32)
             rows_v[i, j : j + 1] = jnp.sum(jnp.where(mine, rows, 0.0), axis=0, keepdims=True).astype(jnp.int32)
         pltpu.make_async_copy(rows_v.at[i], rows_s.at[i], rows_sem.at[i]).start()
 
@@ -263,11 +265,11 @@
             def _():
                 send_own(to * NY + y)
 
-    def send_at(at, now=True):
+    def send_at(at):
         for here in range(NZ):
             if at in SENDS[here]:
 
-                @pl.when((z == here) & now)
+                @pl.when(z == here)
                 def _(here=here):
                     for kind, what in SENDS[here][at]:
                         if kind == "y":
@@ -282,38 +284,43 @@
     for load in loads:
         load.wait()
 
+    def early(i):
+        low, high = (sum((i == k).astype(jnp.int32) for k in range(1, NZ) if at[k] < k) for at in ROWS_AT)
+        return jnp.where(z < HALF, low, high) == 1
+
     def step(i, _):
+        @pl.when(i > 0)
+        def _():
+            base = choose(bases, i - 1)
+            for j in range(NY):
+                send_score(base + j)
+
         for at in range(NZ):
-            send_at(at, i == at)
-
-        @pl.when(i > 0)
-        def _():
-            for j in range(NY):
-                send_score(plane(i - 1, z) * NY + j)
-
-        rows_at = jnp.where(z < HALF, choose(ROWS_AT[0], i), choose(ROWS_AT[1], i))
-        later = jnp.minimum(i + 1, NZ - 1)
-        later_at = jnp.where(z < HALF, choose(ROWS_AT[0], later), choose(ROWS_AT[1], later))
-
-        @pl.when(rows_at == i)
+            if any(at in SENDS[here] for here in range(NZ)):
+
+                @pl.when(i == at)
+                def _(at=at):
+                    send_at(at)
+
+        @pl.when((i > 0) & jnp.logical_not(early(i)))
         def _():
             unpack_rows(i)
 
-        @pl.when((i + 1 < NZ) & (later_at == i))
+        @pl.when(early(i + 1))
         def _():
             unpack_rows(i + 1)
 
-        for dy in range(1, NY):
-            wait_block(plane(i, z) * NY + (y + dy) % NY)
+        base = choose(bases, i)
+        for other in others_y:
+            wait_block(base + other)
         pltpu.make_async_copy(rows_v.at[i], rows_s.at[i], rows_sem.at[i]).wait()
         for j in range(NY):
-            s = plane(i, z) * NY + j
-            score_out[s] = score_block(held[s], lambda k, j=j: rows_s[i, j, k], corpus)
+            score_out[base + j] = score_block(held[base + j], lambda k, j=j: rows_s[i, j, k], corpus)
         return 0
 
     lax.fori_loop(0, NZ, step, 0)
     for j in range(NY):
-        send_score(plane(NZ - 1, z) * NY + j)
+        send_score(bases[NZ - 1] + j)
     others = pl.ds(0, N - 1)
     pltpu.make_async_copy(score_in.at[others], score_in.at[others], s_recv).wait()
     score_in[me] = score_out[me]

time: 44.3 us -> 43.1 us (0.973)
  Pallas kernels: 42.5 us -> 41.1 us
    pallas_call x1, Pallas kernels: 42.5 us -> 41.1 us  [body(): pl.pallas_call(kernel, out_shape=jax.ShapeDtypeStruct((count, N, CAP), jn...]
where the time goes in v4:
time: 43.1 us; the launch traced here: 42.7 us
  Pallas kernels  41.1 us (95%)
  other arithmetic  1.56 us (4%)
    pallas_call x1, Pallas kernels, body(): pl.pallas_call(kernel, out_shape=jax.ShapeDtypeStruct((count, N, CAP), jn...  41.1 us
    select_n x1, other arithmetic, body(): return jnp.where(live, returned, jnp.float32(0.0))  1.56 us

profile of v4, /device:TPU:4, one launch (start us, length us, event | category | flops | bytes accessed | tf_op | source)
XLA Modules:
  0.0 42.7 jit_solution(15822297502649029152)
XLA Ops:
  0.0 41.1 %maxsim.1 = f32[4,32,32]{2,1,0:T(8,128)} custom-call(bf16[128,128]{1,0:T(8,128)(2,1)} %bitcast.1, bf16[256,72,128]{2,1,0:T(8,128)(2,1)} %passages.1, s32[4,32,32]{2,1,0:T(8,128)} %cand_rows.1), custom_call_target="tpu_custom_call" | custom-call | flops 2415919104 | bytes 6291456 | tf_op jit(solution)/shard_map/maxsim/pallas_call | solution.py:341
  41.1 1.6 %fusion = f32[4,32,32]{2,1,0:T(8,128)} fusion(f32[4,32,32]{2,1,0:T(8,128)} %maxsim.1, s32[4,32]{1,0:T(4,128)} %param.7), kind=kLoop, calls=%fused_computation.1 | loop fusion | flops 8192 | bytes 33280 | tf_op jit(solution)/shard_map/jit(_where)/select_n | solution.py:365

commit v5 on v4

--- a/solution.py
+++ b/solution.py
@@ -183,6 +183,21 @@
     queries_in = pltpu.make_async_copy(queries, held.at[me], in_sem.at[1])
     rows_in.start()
     queries_in.start()
+    barrier = pltpu.get_barrier_semaphore()
+    for d in range(1, NZ):
+        to = (z + d) % NZ
+
+        @pl.when(to > z)
+        def _():
+            pl.semaphore_signal(barrier, inc=1, device_id={"shard": to * NY + y}, device_id_type=MESH)
+
+    for d in range(1, NY):
+        to = (y + d) % NY
+
+        @pl.when(to > y)
+        def _():
+            pl.semaphore_signal(barrier, inc=1, device_id={"shard": z * NY + to}, device_id_type=MESH)
+
     loads = []
     part = passages.shape[0] // 4
     for k in range(4):
@@ -190,20 +205,21 @@
         loads.append(pltpu.make_async_copy(passages.at[span], corpus.at[span], load_sem.at[k]))
         loads[-1].start()
 
-    barrier = pltpu.get_barrier_semaphore()
-    for d in range(1, NZ):
-        to = (z + d) % NZ
-
-        @pl.when(to > z)
-        def _():
-            pl.semaphore_signal(barrier, inc=1, device_id={"shard": to * NY + y}, device_id_type=MESH)
-
-    for d in range(1, NY):
-        to = (y + d) % NY
-
-        @pl.when(to > y)
-        def _():
-            pl.semaphore_signal(barrier, inc=1, device_id={"shard": z * NY + to}, device_id_type=MESH)
+    @pl.when(me > 0)
+    def _():
+        pl.semaphore_wait(barrier, z + y)
+
+    for to in range(NY):
+
+        @pl.when(to < y)
+        def _():
+            pl.semaphore_signal(ready_y.at[y], inc=1, device_id={"shard": z * NY + to}, device_id_type=MESH)
+
+    for to in range(NZ):
+
+        @pl.when(to < z)
+        def _():
+            pl.semaphore_signal(ready_z.at[z], inc=1, device_id={"shard": to * NY + y}, device_id_type=MESH)
 
     rows_in.wait()
     packed = jnp.concatenate([own_rows[q] for q in range(4)], axis=1).astype(jnp.float32)
@@ -212,22 +228,6 @@
         own_for[to] = piece.astype(jnp.bfloat16)
     held_rows[me] = own_for[z]
     queries_in.wait()
-
-    @pl.when(me > 0)
-    def _():
-        pl.semaphore_wait(barrier, z + y)
-
-    for to in range(NY):
-
-        @pl.when(to < y)
-        def _():
-            pl.semaphore_signal(ready_y.at[y], inc=1, device_id={"shard": z * NY + to}, device_id_type=MESH)
-
-    for to in range(NZ):
-
-        @pl.when(to < z)
-        def _():
-            pl.semaphore_signal(ready_z.at[z], inc=1, device_id={"shard": to * NY + y}, device_id_type=MESH)
 
     for d in (1, 3, 2):
         to = apart(y, d)

time: 43.1 us -> 41.6 us (0.965)
  Pallas kernels: 41.1 us -> 39.4 us
    pallas_call x1, Pallas kernels: 41.1 us -> 39.4 us  [body(): pl.pallas_call(kernel, out_shape=jax.ShapeDtypeStruct((count, N, CAP), jn...]
where the time goes in v5:
time: 41.6 us; the launch traced here: 41 us
  Pallas kernels  39.4 us (95%)
  other arithmetic  1.56 us (4%)
    pallas_call x1, Pallas kernels, body(): pl.pallas_call(kernel, out_shape=jax.ShapeDtypeStruct((count, N, CAP), jn...  39.4 us
    select_n x1, other arithmetic, body(): return jnp.where(live, returned, jnp.float32(0.0))  1.56 us

profile of v5, /device:TPU:4, one launch (start us, length us, event | category | flops | bytes accessed | tf_op | source)
XLA Modules:
  0.0 41.0 jit_solution(2289822935357804403)
XLA Ops:
  0.0 39.4 %maxsim.1 = f32[4,32,32]{2,1,0:T(8,128)} custom-call(bf16[128,128]{1,0:T(8,128)(2,1)} %bitcast.1, bf16[256,72,128]{2,1,0:T(8,128)(2,1)} %passages.1, s32[4,32,32]{2,1,0:T(8,128)} %cand_rows.1), custom_call_target="tpu_custom_call" | custom-call | flops 2415919104 | bytes 6291456 | tf_op jit(solution)/shard_map/maxsim/pallas_call | solution.py:341
  39.4 1.6 %fusion = f32[4,32,32]{2,1,0:T(8,128)} fusion(f32[4,32,32]{2,1,0:T(8,128)} %maxsim.1, s32[4,32]{1,0:T(4,128)} %param.7), kind=kLoop, calls=%fused_computation.1 | loop fusion | flops 8192 | bytes 33280 | tf_op jit(solution)/shard_map/jit(_where)/select_n | solution.py:365

commit v6 on v5

--- a/solution.py
+++ b/solution.py
@@ -24,32 +24,32 @@
 )
 SENDS = (
     {
-        -1: (("y", 3), ("o", (0, 3)), ("y", 1), ("y", 2), ("o", (0, 2)), ("o", (1, 3)),),
-        0: (("s", 1), ("o", (1, 1)), ("s", 3), ("o", (0, 1)),),
+        -1: (("y", 3), ("o", (0, 3)), ("y", 1), ("y", 2), ("o", (0, 2)), ("o", (1, 3)), ("s", 1),),
+        0: (("o", (1, 1)), ("s", 3), ("o", (0, 1)),),
         1: (("o", (1, 2)), ("s", 2), ("o", (1, 0)),),
         2: (("s", 6), ("s", 4),),
         3: (("s", 5),),
         4: (("s", 7),),
     },
     {
-        -1: (("y", 3), ("o", (0, 3)), ("y", 1), ("y", 2), ("o", (0, 2)), ("o", (1, 3)),),
-        0: (("s", 1), ("o", (1, 1)), ("s", 3), ("o", (0, 1)),),
+        -1: (("y", 3), ("o", (0, 3)), ("y", 1), ("y", 2), ("o", (0, 2)), ("o", (1, 3)), ("s", 1),),
+        0: (("o", (1, 1)), ("s", 3), ("o", (0, 1)),),
         1: (("o", (1, 2)), ("s", 2), ("o", (1, 0)),),
         2: (("s", 6), ("s", 4),),
         3: (("s", 5),),
         4: (("s", 7),),
     },
     {
-        -1: (("y", 3), ("o", (0, 3)), ("y", 1), ("y", 2), ("o", (0, 2)), ("o", (1, 3)),),
-        0: (("s", 1), ("o", (1, 1)), ("s", 3), ("o", (0, 1)),),
+        -1: (("y", 3), ("o", (0, 3)), ("y", 1), ("y", 2), ("o", (0, 2)), ("o", (1, 3)), ("s", 1),),
+        0: (("o", (1, 1)), ("s", 3), ("o", (0, 1)),),
         1: (("o", (1, 2)), ("s", 2), ("o", (1, 0)),),
         2: (("s", 6), ("s", 4),),
         3: (("s", 5),),
         4: (("s", 7),),
     },
     {
-        -1: (("y", 3), ("o", (0, 3)), ("y", 1), ("y", 2), ("o", (0, 2)), ("o", (1, 3)),),
-        0: (("s", 1), ("o", (1, 1)), ("s", 3), ("o", (0, 1)),),
+        -1: (("y", 3), ("o", (0, 3)), ("y", 1), ("y", 2), ("o", (0, 2)), ("o", (1, 3)), ("s", 1),),
+        0: (("o", (1, 1)), ("s", 3), ("o", (0, 1)),),
         1: (("o", (1, 2)), ("s", 2), ("o", (1, 0)),),
         2: (("s", 6), ("s", 4),),
         3: (("s", 5),),
@@ -169,13 +169,16 @@
         for dy in (2, 1, 3):
             send(held_rows.at[s], s, z * NY + others_y[dy - 1])
 
+    def member(i, j):
+        return jnp.where(y == j, choose(bases[1:] + bases[-1:], i), choose(bases, i)) + j
+
     def unpack_rows(i):
-        base = choose(bases, i)
+        base = bases[i] if isinstance(i, int) else choose(bases, i)
         for other in others_y:
             wait_rows(base + other)
         mine = lax.broadcasted_iota(jnp.int32, (16, LANES), 0) == y
         for j in range(NY):
-            rows = held_rows[base + j].astype(jnp.float32)
+            rows = held_rows[member(i, j)].astype(jnp.float32)
             rows_v[i, j : j + 1] = jnp.sum(jnp.where(mine, rows, 0.0), axis=0, keepdims=True).astype(jnp.int32)
         pltpu.make_async_copy(rows_v.at[i], rows_s.at[i], rows_sem.at[i]).start()
 
@@ -279,10 +282,17 @@
                         else:
                             spread(what)
 
+    mine = lax.broadcasted_iota(jnp.int32, (16, LANES), 0) == y
+    own_row = jnp.sum(jnp.where(mine, held_rows[me].astype(jnp.float32), 0.0), axis=0, keepdims=True)
+    rows_v[NZ] = jnp.broadcast_to(own_row.astype(jnp.int32), (NY, LANES))
+    own_in = pltpu.make_async_copy(rows_v.at[NZ], rows_s.at[NZ], rows_sem.at[NZ])
+    own_in.start()
+    for load in loads:
+        load.wait()
+    own_in.wait()
+    score_out[me] = score_block(held[me], lambda k: rows_s[NZ, 0, k], corpus)
     send_at(-1)
     unpack_rows(0)
-    for load in loads:
-        load.wait()
 
     def early(i):
         low, high = (sum((i == k).astype(jnp.int32) for k in range(1, NZ) if at[k] < k) for at in ROWS_AT)
@@ -291,9 +301,8 @@
     def step(i, _):
         @pl.when(i > 0)
         def _():
-            base = choose(bases, i - 1)
             for j in range(NY):
-                send_score(base + j)
+                send_score(member(i - 1, j))
 
         for at in range(NZ):
             if any(at in SENDS[here] for here in range(NZ)):
@@ -310,17 +319,27 @@
         def _():
             unpack_rows(i + 1)
 
-        base = choose(bases, i)
+        await_others(choose(bases, i))
+        pltpu.make_async_copy(rows_v.at[i], rows_s.at[i], rows_sem.at[i]).wait()
+        for j in range(NY):
+            score_out[member(i, j)] = score_block(held[member(i, j)], lambda k, j=j: rows_s[i, j, k], corpus)
+        return 0
+
+    def await_others(base):
         for other in others_y:
             wait_block(base + other)
-        pltpu.make_async_copy(rows_v.at[i], rows_s.at[i], rows_sem.at[i]).wait()
-        for j in range(NY):
-            score_out[base + j] = score_block(held[base + j], lambda k, j=j: rows_s[i, j, k], corpus)
-        return 0
-
-    lax.fori_loop(0, NZ, step, 0)
+
+    last = NZ - 1
+    lax.fori_loop(0, last, step, 0)
     for j in range(NY):
-        send_score(bases[NZ - 1] + j)
+        send_score(member(last - 1, j))
+    await_others(bases[last])
+    pltpu.make_async_copy(rows_v.at[last], rows_s.at[last], rows_sem.at[last]).wait()
+    for other in others_y:
+        s = bases[last] + other
+        score_out[s] = score_block(held[s], lambda k, other=other: rows_s[last, other, k], corpus)
+    for other in others_y:
+        send_score(bases[last] + other)
     others = pl.ds(0, N - 1)
     pltpu.make_async_copy(score_in.at[others], score_in.at[others], s_recv).wait()
     score_in[me] = score_out[me]
@@ -348,12 +367,12 @@
             pltpu.VMEM((N, 16, LANES), jnp.bfloat16),
             pltpu.VMEM((NZ, 16, LANES), jnp.bfloat16),
             pltpu.VMEM(passages.shape, jnp.bfloat16),
-            pltpu.VMEM((NZ, NY, LANES), jnp.int32),
-            pltpu.SMEM((NZ, NY, LANES), jnp.int32),
+            pltpu.VMEM((NZ + 1, NY, LANES), jnp.int32),
+            pltpu.SMEM((NZ + 1, NY, LANES), jnp.int32),
             pltpu.VMEM((N, 1, LANES), jnp.float32),
             pltpu.VMEM((N, 1, LANES), jnp.float32),
             pltpu.VMEM(cand_rows.shape, jnp.int32),
-            dma((4,)), dma((2,)), dma((NZ,)),
+            dma((4,)), dma((2,)), dma((NZ + 1,)),
             dma, dma((N,)), dma, dma((N,)), dma, dma,
             regular((NZ,)), regular((NY,)),
         ],

time: 41.6 us -> 41.1 us (0.988)
  no operation moved by 1% of the time
where the time goes in v6:
time: 41.1 us; the launch traced here: 40.7 us
  Pallas kernels  39.1 us (95%)
  other arithmetic  1.56 us (4%)
    pallas_call x1, Pallas kernels, body(): pl.pallas_call(kernel, out_shape=jax.ShapeDtypeStruct((count, N, CAP), jn...  39.1 us
    select_n x1, other arithmetic, body(): return jnp.where(live, returned, jnp.float32(0.0))  1.56 us

profile of v6, /device:TPU:4, one launch (start us, length us, event | category | flops | bytes accessed | tf_op | source)
XLA Modules:
  0.0 40.7 jit_solution(4849214954830711034)
XLA Ops:
  0.0 39.1 %maxsim.1 = f32[4,32,32]{2,1,0:T(8,128)} custom-call(bf16[128,128]{1,0:T(8,128)(2,1)} %bitcast.1, bf16[256,72,128]{2,1,0:T(8,128)(2,1)} %passages.1, s32[4,32,32]{2,1,0:T(8,128)} %cand_rows.1), custom_call_target="tpu_custom_call" | custom-call | flops 2415919104 | bytes 6291456 | tf_op jit(solution)/shard_map/maxsim/pallas_call | solution.py:360
  39.1 1.6 %fusion = f32[4,32,32]{2,1,0:T(8,128)} fusion(f32[4,32,32]{2,1,0:T(8,128)} %maxsim.1, s32[4,32]{1,0:T(4,128)} %param.7), kind=kLoop, calls=%fused_computation.1 | loop fusion | flops 8192 | bytes 33280 | tf_op jit(solution)/shard_map/jit(_where)/select_n | solution.py:384

commit v7 on v6

--- a/solution.py
+++ b/solution.py
@@ -156,11 +156,9 @@
         pltpu.make_async_copy(held.at[s], held.at[s], q_recv.at[s]).wait()
 
     def send_score(s):
-        @pl.when(s != me)
-        def _():
-            pltpu.make_async_remote_copy(
-                src_ref=score_out.at[s], dst_ref=score_in.at[me], send_sem=s_send, recv_sem=s_recv,
-                device_id={"shard": s}, device_id_type=MESH).start()
+        pltpu.make_async_remote_copy(
+            src_ref=score_out.at[s], dst_ref=score_in.at[me], send_sem=s_send, recv_sem=s_recv,
+            device_id={"shard": s}, device_id_type=MESH).start()
 
     def spread(i):
         s = bases[i] + y
@@ -321,8 +319,9 @@
 
         await_others(choose(bases, i))
         pltpu.make_async_copy(rows_v.at[i], rows_s.at[i], rows_sem.at[i]).wait()
-        for j in range(NY):
-            score_out[member(i, j)] = score_block(held[member(i, j)], lambda k, j=j: rows_s[i, j, k], corpus)
+        shards = [member(i, j) for j in range(NY)]
+        for j, s in enumerate(shards):
+            score_out[s] = score_block(held[s], lambda k, j=j: rows_s[i, j, k], corpus)
         return 0
 
     def await_others(base):

time: 41.1 us -> 41.1 us (level)
  no operation moved by 1% of the time
where the time goes in v7:
time: 41.1 us; the launch traced here: 40.6 us
  Pallas kernels  39.1 us (95%)
  other arithmetic  1.56 us (4%)
    pallas_call x1, Pallas kernels, body(): pl.pallas_call(kernel, out_shape=jax.ShapeDtypeStruct((count, N, CAP), jn...  39.1 us
    select_n x1, other arithmetic, body(): return jnp.where(live, returned, jnp.float32(0.0))  1.56 us

profile of v7, /device:TPU:4, one launch (start us, length us, event | category | flops | bytes accessed | tf_op | source)
XLA Modules:
  0.0 40.6 jit_solution(12322591947574895171)
XLA Ops:
  0.0 39.1 %maxsim.1 = f32[4,32,32]{2,1,0:T(8,128)} custom-call(bf16[128,128]{1,0:T(8,128)(2,1)} %bitcast.1, bf16[256,72,128]{2,1,0:T(8,128)(2,1)} %passages.1, s32[4,32,32]{2,1,0:T(8,128)} %cand_rows.1), custom_call_target="tpu_custom_call" | custom-call | flops 2415919104 | bytes 6291456 | tf_op jit(solution)/shard_map/maxsim/pallas_call | solution.py:359
  39.1 1.6 %fusion = f32[4,32,32]{2,1,0:T(8,128)} fusion(f32[4,32,32]{2,1,0:T(8,128)} %maxsim.1, s32[4,32]{1,0:T(4,128)} %param.7), kind=kLoop, calls=%fused_computation.1 | loop fusion | flops 8192 | bytes 33280 | tf_op jit(solution)/shard_map/jit(_where)/select_n | solution.py:383
